TPU v7x, 32 devices: a whole 2x2x4 slice. The times are simulated.
32 devices in a mesh: ha: 4 (over y, x), wa: 8 (over z, core).
Axes of the slice: x: 2, y: 2, z: 4, core: 2. Of those that a mesh axis runs over, the one named last changes fastest.
Arguments:
- tokens: bfloat16 [4, 32, 64, 1536], P(None, 'ha', 'wa'), may hold values from -6 to 6
- shift: float32 [1536], replicated, may hold values from -3 to 3
- scale: float32 [1536], replicated, may hold values from -3 to 3
- gate: float32 [1536], replicated, may hold values from -4 to 4
- qkv_weight: bfloat16 [1536, 4608], P('wa'), may hold values from -0.17860863 to 0.17860863
- out_weight: bfloat16 [1536, 1536], P('wa'), may hold values from -0.15625 to 0.15625
- q_gain: float32 [128], replicated, may hold values from 1.4 to 6.5
- k_gain: float32 [128], replicated, may hold values from 1.4 to 6.5
Outputs:
- update: bfloat16 [4, 32, 64, 1536], P(None, 'ha', 'wa')
All inputs are finite; a program needn't handle non-finite values.
Results may differ from a plain program's by a relative error of at most 0.009.
The roundings to bfloat16 on the way count: a program that leaves them out, or rounds other values in their place, can miss the bound.
Values may be sent and summed in bfloat16 or wider, within the bound.
A program may use at most 128 MiB of HBM per device.

v0:
```python
import jax
import jax.numpy as jnp
from jax import lax
from jax.sharding import PartitionSpec as P

HEADS = 12
HD = 128
TILE_T = 4


def padded(x, sides, width):
    for axis, dim in sides:
        peers, length = (lax.axis_size(axis), x.shape[dim])
        up = [(i, (i + 1) % peers) for i in range(peers - 1)]
        down = [(j, i) for i, j in up]
        last = lax.slice_in_dim(x, length - width, length, axis=dim)
        initial = lax.slice_in_dim(x, 0, width, axis=dim)
        before = lax.ppermute(last, axis, up)
        after = lax.ppermute(initial, axis, down)
        x = jnp.concatenate([before, x, after], axis=dim)
    return x


def add_rows(left, piece):
    return jnp.dot(left, piece, preferred_element_type=jnp.float32)


def per_head_norm(raw, gain):
    return (raw * lax.rsqrt(jnp.mean(raw * raw, axis=-1, keepdims=True) + 1e-06) * gain).astype(
        jnp.bfloat16
    )


def shards(tokens, shift, scale, gate, qkv_weight, out_weight, q_gain, k_gain):
    frame_list, tile_h, tile_w, width = tokens.shape
    count = frame_list * tile_h * tile_w
    inner = HEADS * HD
    groups = frame_list // TILE_T
    tall = lax.axis_size("ha")
    wide = lax.axis_size("wa")
    flat = tokens.reshape(count, width).astype(jnp.float32)
    mean = jnp.mean(flat, axis=-1, keepdims=True)
    centred = flat - mean
    var = jnp.mean(centred * centred, axis=-1, keepdims=True)
    normed = centred / jnp.sqrt(var + 1e-06)
    modulated = (normed * (1.0 + scale) + shift).astype(jnp.bfloat16)
    projected = add_rows(modulated, lax.all_gather(qkv_weight, "wa", axis=0, tiled=True))
    query = per_head_norm(projected[:, :inner].reshape(count, HEADS, HD), q_gain)
    key = per_head_norm(projected[:, inner : 2 * inner].reshape(count, HEADS, HD), k_gain)
    value = projected[:, 2 * inner :].astype(jnp.bfloat16)
    both = jnp.concatenate(
        [
            key.reshape(frame_list, tile_h, tile_w, inner),
            value.reshape(frame_list, tile_h, tile_w, inner),
        ],
        axis=-1,
    )
    window = padded(both, (("ha", 1), ("wa", 2)), tile_h)
    rows = lax.axis_index("ha") * tile_h - tile_h + jnp.arange(3 * tile_h, dtype=jnp.int32)
    cols = lax.axis_index("wa") * tile_w - tile_w + jnp.arange(3 * tile_w, dtype=jnp.int32)
    rows_ok = (rows >= 0) & (rows < tile_h * tall)
    cols_ok = (cols >= 0) & (cols < tile_w * wide)
    valid = jnp.broadcast_to(
        rows_ok[:, None] & cols_ok[None, :], (TILE_T, 3 * tile_h, 3 * tile_w)
    ).reshape(-1)
    window = window.reshape(groups, -1, 2 * inner)
    keys = window[:, :, :inner].reshape(groups, -1, HEADS, HD)
    values = window[:, :, inner:].reshape(groups, -1, HEADS, HD)
    queries = query.reshape(groups, -1, HEADS, HD)
    inv_root = 1.0 / jnp.sqrt(jnp.float32(HD))

    def one_head(head):
        query_head_rows = lax.dynamic_index_in_dim(queries, head, 2, keepdims=False)
        key_head_rows = lax.dynamic_index_in_dim(keys, head, 2, keepdims=False)
        value_head_rows = lax.dynamic_index_in_dim(values, head, 2, keepdims=False)
        scores = (
            jnp.einsum(
                "nur,ncr->nuc", query_head_rows, key_head_rows, preferred_element_type=jnp.float32
            )
            * inv_root
        )
        scores = jnp.where(valid[None, None, :], scores, -jnp.inf)
        top = jnp.max(scores, axis=-1, keepdims=True)
        expo = jnp.exp(scores - top)
        total = jnp.sum(expo, axis=-1, keepdims=True)
        probability_rows = expo.astype(jnp.bfloat16)
        summed_output = jnp.einsum(
            "ypi,yif->ypf", probability_rows, value_head_rows, preferred_element_type=jnp.float32
        )
        return summed_output / total

    per_head = lax.map(one_head, jnp.arange(HEADS, dtype=jnp.int32))
    attended = jnp.transpose(per_head, (1, 2, 0, 3)).reshape(count, inner).astype(jnp.bfloat16)
    output = add_rows(attended, lax.all_gather(out_weight, "wa", axis=0, tiled=True))
    return (gate * output).astype(jnp.bfloat16).reshape(frame_list, tile_h, tile_w, width)


def solution(mesh):
    return jax.shard_map(
        shards,
        mesh=mesh,
        in_specs=(P(None, "ha", "wa", None), P(), P(), P(), P("wa", None), P("wa", None), P(), P()),
        out_specs=P(None, "ha", "wa", None),
        check_vma=False,
    )
```

profile of v0, /device:TPU:12, one launch (start us, length us, event | category | flops | bytes accessed | tf_op | source)
XLA Modules:
  0.0 450.0 jit_solution(1388491029669792274)
XLA Ops:
  9.6 127.4 %all-gather.3.cloned.1.call-done = bf16[1536,4608]{1,0:T(8,128)(2,1)} async-done(((bf16[192,4608]{1,0:T(8,128)(2,1)}), bf16[1536,4608]{1,0:T(8,128)(2,1)}) %all-gather.3.cloned.1.call-update) | async-done | bytes 14155792 | tf_op jit(solution)/shard_map/all_gather | solution.py:47
  137.0 7.0 %fusion.29 = f32[256,4608]{1,0:T(8,128)S(1)} fusion(bf16[256,1536]{1,0:T(8,128)(2,1)S(1)} %fusion.26, bf16[1536,4608]{1,0:T(8,128)(2,1)} %all-gather.3.cloned.1.call-done), kind=kOutput, calls=%fused_computation.47 | convolution fusion | flops 3623878656 | bytes 19660800 | tf_op jit(solution)/shard_map/dot_general | solution.py:25
  144.1 2.5 slice_multiply_fusion
  146.7 1.6 copy.11
  152.0 2.2 multiply_convert_fusion
  154.3 3.4 collective-permute-start.1
  157.7 2.6 collective-permute-start
  160.3 32.5 %collective-permute-done.1 = bf16[4,8,8,3072]{3,2,1,0:T(8,128)(2,1)S(1)} collective-permute-done((bf16[4,8,8,3072]{3,2,1,0:T(8,128)(2,1)S(1)}, bf16[4,8,8,3072]{3,2,1,0:T(8,128)(2,1)S(1)}, u32[]{:S(2)}, u32[]{:S(2)}) %collective-permute-start.1) | collective-permute-done | bytes 1572896 | tf_op jit(solution)/shard_map/ppermute | solution.py:19
  192.8 33.5 %collective-permute-done = bf16[4,8,8,3072]{3,2,1,0:T(8,128)(2,1)S(1)} collective-permute-done((bf16[4,8,8,3072]{3,2,1,0:T(8,128)(2,1)S(1)}, bf16[4,8,8,3072]{3,2,1,0:T(8,128)(2,1)S(1)}, u32[]{:S(2)}, u32[]{:S(2)}) %collective-permute-start) | collective-permute-done | bytes 1572896 | tf_op jit(solution)/shard_map/ppermute | solution.py:18
  226.2 2.7 pad_maximum_fusion.1
  228.9 4.5 collective-permute-start.3
  233.4 1.9 collective-permute-start.2
  235.5 3.0 copy.9
  238.5 3.0 copy.10
  241.5 1.5 reduce_sum.47
  243.1 2.8 multiply_convert_fusion.1
  245.9 77.3 %collective-permute-done.3 = bf16[4,24,8,3072]{3,2,1,0:T(8,128)(2,1)} collective-permute-done((bf16[4,24,8,3072]{3,2,1,0:T(8,128)(2,1)}, bf16[4,24,8,3072]{3,2,1,0:T(8,128)(2,1)}, u32[]{:S(2)}, u32[]{:S(2)}) %collective-permute-start.3) | collective-permute-done | bytes 4718624 | tf_op jit(solution)/shard_map/ppermute | solution.py:19
  323.3 3.8 collective-permute-done.2
  327.1 6.8 %pad_maximum_fusion = bf16[4,24,24,3072]{3,2,1,0:T(8,128)(2,1)S(1)} fusion(bf16[4,24,8,3072]{3,2,1,0:T(8,128)(2,1)} %collective-permute-done.3, bf16[4,8,8,3072]{3,2,1,0:T(8,128)(2,1)S(1)} %collective-permute-done.1, bf16[4,8,8,1536]{3,2,1,0:T(8,128)(2,1)S(1)} %bitcast.62, bf16[4,8,8,1536]{3,2,1,0:T(8,128)(2,1)S(1)} %multiply_convert_fusion, ...), kind=kLoop, calls=%fused_computation.19 | loop fusion | flops 84934656 | bytes 28311552 | tf_op jit(solution)/shard_map/concatenate | solution.py:20
  333.9 5.3 %fusion.28 = (bf16[1,2304,1536]{2,1,0:T(8,128)(2,1)}, bf16[1,2304,1536]{2,1,0:T(8,128)(2,1)}) fusion(bf16[1,2304,3072]{2,1,0:T(8,128)(2,1)S(1)} %bitcast.57), kind=kLoop, calls=%fused_computation.46 | loop fusion | bytes 28311552 | tf_op jit(solution)/shard_map/slice | solution.py:68
  339.2 10.4 %copy.24 = bf16[1,2304,1536]{1,2,0:T(8,128)(2,1)} copy(bf16[1,2304,1536]{2,1,0:T(8,128)(2,1)} %get-tuple-element.84) | data formatting | bytes 14155776
  349.6 10.2 %copy.25 = bf16[1,2304,1536]{1,2,0:T(8,128)(2,1)} copy(bf16[1,2304,1536]{2,1,0:T(8,128)(2,1)} %get-tuple-element.83) | data formatting | bytes 14155776
  359.7 78.7 %while.11 = (s32[]{:T(128)}, bf16[12,1,256,128]{2,3,0,1:T(8,128)(2,1)S(1)}, s32[12]{0:T(128)S(1)}, bf16[1,256,12,128]{1,3,2,0:T(8,128)(2,1)}, bf16[1,2304,12,128...) while((s32[]{:T(128)}, ...), condition=%wide.region_7.8_spmd.clone, body=%wide.region_4.7_spmd.clone.sunk | while | flops 306183680 | bytes 8666851 | solution.py:92
  362.4 1.7 fusion.41
  364.6 1.6 fusion.43
  368.9 1.7 fusion.41
  371.1 1.6 fusion.43
  375.5 1.7 fusion.41
  377.7 1.6 fusion.43
  382.1 1.7 fusion.41
  384.2 1.6 fusion.43
  388.6 1.7 fusion.41
  390.8 1.6 fusion.43
  395.2 1.7 fusion.41
  397.3 1.6 fusion.43
  401.7 1.7 fusion.41
  403.9 1.6 fusion.43
  408.3 1.7 fusion.41
  410.5 1.6 fusion.43
  414.9 1.7 fusion.41
  417.0 1.6 fusion.43
  421.4 1.7 fusion.41
  423.6 1.6 fusion.43
  428.0 1.7 fusion.41
  430.1 1.6 fusion.43
  434.5 1.7 fusion.41
  436.7 1.6 fusion.43
  438.5 4.6 %fusion.22 = bf16[256,1536]{1,0:T(8,128)(2,1)} fusion(bf16[256,1536]{0,1:T(8,128)(2,1)S(1)} %bitcast.67, bf16[1536,1536]{1,0:T(8,128)(2,1)} %all-gather.5.cloned.1.call-done, f32[1536]{0:T(1024)S(1)} %copy-done.9), kind=kOutput, calls=%fused_computation.22 | convolution fusion | flops 1208745984 | bytes 6297600 | tf_op jit(solution)/shard_map/dot_general | solution.py:25
  (118 shorter events, 22.5 us)
Async XLA Ops:
  6.5 2.7 copy-start
  6.5 2.2 copy-start.2
  6.5 2.7 copy-start.6
  6.5 2.7 copy-start.5
  6.5 130.5 %all-gather.3.cloned.1.call-start = ((), (), s32[]{:S(2)}) async-start(), calls=%async_computation | async-start | bytes 15925248 | tf_op jit(solution)/shard_map/all_gather | solution.py:47
  7.3 431.2 %all-gather.5.cloned.1.call-start = ((), (), s32[]{:S(2)}) async-start(), calls=%async_computation.1 | async-start | bytes 5308416 | tf_op jit(solution)/shard_map/all_gather | solution.py:94
  154.3 38.5 %collective-permute-start.1 = (bf16[4,8,8,3072]{3,2,1,0:T(8,128)(2,1)S(1)}, bf16[4,8,8,3072]{3,2,1,0:T(8,128)(2,1)S(1)}, u32[]{:S(2)}, u32[]{:S(2)}) collective-permute-start(bf16[4,8,8,3072]{3,2,1,0:T(8,128)(2,1)S(1)} %pad_maximum_fusion.2), channel_id=1, source_target_pairs={{8,0},{16,8},{24,16},{9,1},{17,9},{25,17},{10,2},{18,10},{26,18},{... | collective-permute-start | bytes 4718600 | tf_op jit(solution)/shard_map/ppermute | solution.py:19
  157.7 68.5 %collective-permute-start = (bf16[4,8,8,3072]{3,2,1,0:T(8,128)(2,1)S(1)}, bf16[4,8,8,3072]{3,2,1,0:T(8,128)(2,1)S(1)}, u32[]{:S(2)}, u32[]{:S(2)}) collective-permute-start(bf16[4,8,8,3072]{3,2,1,0:T(8,128)(2,1)S(1)} %pad_maximum_fusion.2), channel_id=1, source_target_pairs={{0,8},{8,16},{16,24},{1,9},{9,17},{17,25},{2,10},{10,18},{18,26},{... | collective-permute-start | bytes 4718600 | tf_op jit(solution)/shard_map/ppermute | solution.py:18
  226.2 2.7 copy-start.3
  228.9 94.3 %collective-permute-start.3 = (bf16[4,24,8,3072]{3,2,1,0:T(8,128)(2,1)}, bf16[4,24,8,3072]{3,2,1,0:T(8,128)(2,1)}, u32[]{:S(2)}, u32[]{:S(2)}) collective-permute-start(bf16[4,24,8,3072]{3,2,1,0:T(8,128)(2,1)} %pad_maximum_fusion.1), channel_id=1, source_target_pairs={{1,0},{2,1},{3,2},{4,3},{5,4},{6,5},{7,6},{9,8},{10,9},{11,10},{12... | collective-permute-start | bytes 14155784 | tf_op jit(solution)/shard_map/ppermute | solution.py:19
  233.4 93.7 %collective-permute-start.2 = (bf16[4,24,8,3072]{3,2,1,0:T(8,128)(2,1)}, bf16[4,24,8,3072]{3,2,1,0:T(8,128)(2,1)}, u32[]{:S(2)}, u32[]{:S(2)}) collective-permute-start(bf16[4,24,8,3072]{3,2,1,0:T(8,128)(2,1)} %pad_maximum_fusion.1), channel_id=1, source_target_pairs={{0,1},{1,2},{2,3},{3,4},{4,5},{5,6},{6,7},{8,9},{9,10},{10,11},{11... | collective-permute-start | bytes 14155784 | tf_op jit(solution)/shard_map/ppermute | solution.py:18
  238.5 4.6 %copy-start.7 = (f32[128]{0:T(128)S(1)}, f32[128]{0:T(128)}, u32[]{:S(2)}) copy-start(f32[128]{0:T(128)} %param.16) | copy-start | bytes 1540
  243.1 84.0 %copy-start.4 = (bf16[4,8,8,3072]{3,2,1,0:T(8,128)(2,1)S(1)}, bf16[4,8,8,3072]{3,2,1,0:T(8,128)(2,1)}, u32[]{:S(2)}) copy-start(bf16[4,8,8,3072]{3,2,1,0:T(8,128)(2,1)} %copy-done.3) | copy-start | bytes 4718596
  349.6 10.2 %copy-start.8 = (bf16[12,1,256,128]{2,3,0,1:T(8,128)(2,1)S(1)}, bf16[12,1,256,128]{2,3,0,1:T(8,128)(2,1)}, u32[]{:S(2)}) copy-start(bf16[12,1,256,128]{2,3,0,1:T(8,128)(2,1)} %custom-call) | copy-start | bytes 2359300
  359.7 78.8 %copy-start.9 = (f32[1536]{0:T(1024)S(1)}, f32[1536]{0:T(1024)}, u32[]{:S(2)}) copy-start(f32[1536]{0:T(1024)} %param.13) | copy-start | bytes 18436
  438.5 4.6 %copy-start.1 = (f32[128]{0:T(128)S(1)}, f32[128]{0:T(128)}, u32[]{:S(2)}) copy-start(f32[128]{0:T(128)} %param.17) | copy-start | bytes 1540
Sparse Core Ops, SparseCore 0:
  9.0 127.9 all-gather.2
  235.5 69.2 all-gather.4
where the time goes:
time: 452 us; the launch traced here: 450 us
  waiting for transfers between devices  275 us (61%)
  matrix products  51.1 us (11%)
  local copies, waits for them, and re-layouts  45.6 us (10%)
  other arithmetic  28.1 us (6%)
  loops' own time  23.9 us (5%)
  between operations  13.6 us (3%)
  starting transfers between devices  12.4 us (3%)
    all_gather x1, waiting for transfers between devices, shards(): lax.all_gather(qkv_weight, 'wa', axis=0, tiled=True)  127 us
    ppermute x2, waiting for transfers between devices, padded(): after = lax.ppermute(initial, axis, down)  110 us
    ppermute x2, waiting for transfers between devices, padded(): before = lax.ppermute(last, axis, up)  37.3 us
    another operation x1, loops' own time, shards(): per_head = lax.map(one_head, jnp.arange(HEADS, dtype=jnp.int32))  23.9 us
    unnamed x22, local copies, waits for them, and re-layouts  20.6 us
    dot_general x12, matrix products, one_head(): jnp.einsum('nur,ncr->nuc', query_head_rows, key_head_rows, preferred_elem...  20.3 us
    dot_general x12, matrix products, one_head(): jnp.einsum('ypi,yif->ypf', probability_rows, value_head_rows, preferred_e...  19.1 us
    dot_general x2, matrix products, add_rows(): return jnp.dot(left, piece, preferred_element_type=jnp.float32)  11.7 us
  transfers between devices with their start and end apart: 6, of which 5 were waited for; matrix products, arithmetic and copies ran while one was open for 22% of the time, Pallas kernels for 0%

commit v1 on v0

--- a/solution.py
+++ b/solution.py
@@ -1,6 +1,8 @@
 import jax
 import jax.numpy as jnp
 from jax import lax
+from jax.experimental import pallas as pl
+from jax.experimental.pallas import tpu as pltpu
 from jax.sharding import PartitionSpec as P
 
 HEADS = 12
@@ -31,7 +33,7 @@
     )
 
 
-def shards(tokens, shift, scale, gate, qkv_weight, out_weight, q_gain, k_gain):
+def shards_general(tokens, shift, scale, gate, qkv_weight, out_weight, q_gain, k_gain):
     frame_list, tile_h, tile_w, width = tokens.shape
     count = frame_list * tile_h * tile_w
     inner = HEADS * HD
@@ -95,6 +97,362 @@
     return (gate * output).astype(jnp.bfloat16).reshape(frame_list, tile_h, tile_w, width)
 
 
+def modulate(flat, shift, scale):
+    mean = jnp.mean(flat, axis=-1, keepdims=True)
+    centred = flat - mean
+    var = jnp.mean(centred * centred, axis=-1, keepdims=True)
+    normed = centred / jnp.sqrt(var + 1e-06)
+    return (normed * (1.0 + scale) + shift).astype(jnp.bfloat16)
+
+
+def softmax_step(state, query, keys, values):
+    factor = 1.4426950408889634 * HD**-0.5
+    scores = lax.dot_general(
+        query, keys, (((1,), (1,)), ((), ())), preferred_element_type=jnp.float32
+    )
+    top = jnp.max(scores, axis=-1, keepdims=True) * factor
+    if state is not None:
+        top = jnp.maximum(top, state[0])
+    expo = jnp.exp2(scores * factor - top)
+    total = jnp.sum(expo, axis=-1, keepdims=True)
+    summed = jnp.dot(expo.astype(jnp.bfloat16), values, preferred_element_type=jnp.float32)
+    if state is not None:
+        keep = jnp.exp2(state[0] - top)
+        total = total + keep * state[1]
+        summed = summed + keep * state[2]
+    return top, total, summed
+
+
+MESH = pl.DeviceIdType.MESH
+
+
+def block_kernel(
+    wide, tokens, shift, scale, gate, qkv_weight, out_weight, q_gain, k_gain, update,
+    mod, wbuf, obuf, query, kv, attended, gathered, tops, totals, sums,
+    load_sem, w_send, w_recv, t_send, t_recv, f_send, kv_send, kv_recv,
+    o_send, o_recv, os_send, os_recv, a_send, a_recv,
+):
+    h, w = lax.axis_index("ha"), lax.axis_index("wa")
+    z, c = lax.div(w, 2), lax.rem(w, 2)
+    x, y = lax.rem(h, 2), lax.div(h, 2)
+    deep = wide // 2
+    count, width = tokens.shape
+    half = count // 2
+    depth = qkv_weight.shape[0]
+    mine = wbuf.shape[-1]
+    each = mine // HD
+    inner = HEADS * HD
+    has_left, has_right = z > 0, z < deep - 1
+    ahead, behind, sibling = (h, w + 2), (h, w - 2), (h, w + 1 - 2 * c)
+    peers = [h, 2 * y + 1 - x, 2 * (1 - y) + x, 3 - h]
+    far = (h, w - 1 + 2 * c)
+    has_far = jnp.where(c == 0, z, deep - 1 - z) > 0
+    pending = []
+
+    def remote(src, dst, send, recv, device):
+        return pltpu.make_async_remote_copy(
+            src_ref=src, dst_ref=dst, send_sem=send, recv_sem=recv,
+            device_id=device, device_id_type=MESH,
+        )
+
+    def send(copy, cond=None):
+        if cond is None:
+            copy.start()
+        else:
+            pl.when(cond)(copy.start)
+        pending.append((copy, cond))
+
+    def slot(kind, source):
+        rows = pl.ds(pl.multiple_of(source * depth, 16), depth)
+        return obuf.at[h, rows] if kind == 3 else wbuf.at[kind, rows]
+
+    def load(kind):
+        if kind == 3:
+            source = out_weight.at[:, pl.ds(pl.multiple_of(h * mine, HD), mine)]
+        else:
+            part = (inner, 2 * inner, 0)[kind]
+            source = qkv_weight.at[:, pl.ds(pl.multiple_of(part + h * mine, HD), mine)]
+        return pltpu.make_async_copy(source, slot(kind, w), load_sem.at[kind])
+
+    def pass_on(kind, step, way, device, source):
+        block = slot(kind, source)
+        return remote(
+            block, block, w_send.at[kind, step, way], w_recv.at[kind, source], device
+        )
+
+    def send_own(kind):
+        load(kind).wait()
+        send(pass_on(kind, 0, 0, ahead, w), has_right)
+        send(pass_on(kind, 0, 1, behind, w), has_left)
+        send(pass_on(kind, 0, 2, sibling, w))
+
+    def forward(kind, d):
+        from_left, from_right = z >= d, z < deep - d
+        source = w - 2 * d
+        pl.when(from_left)(pass_on(kind, 2 * d - 1, 2, sibling, source).wait_recv)
+        send(pass_on(kind, 2 * d - 1, 0, ahead, source), from_left & has_right)
+        send(pass_on(kind, 2 * d - 1, 2, sibling, source), from_left)
+        source = w + 2 * d
+        pl.when(from_right)(pass_on(kind, 2 * d, 2, sibling, source).wait_recv)
+        send(pass_on(kind, 2 * d, 1, behind, source), from_right & has_left)
+        send(pass_on(kind, 2 * d, 2, sibling, source), from_right)
+
+    def whole(kind):
+        for i in range(deep):
+            pass_on(kind, 0, 2, sibling, 2 * i + 1 - c).wait_recv()
+
+    for kind in range(4):
+        load(kind).start()
+
+    barrier = pltpu.get_barrier_semaphore()
+
+    def greet(device):
+        pl.semaphore_signal(barrier, inc=1, device_id=device, device_id_type=MESH)
+
+    for peer in peers[1:]:
+        greet((peer, w))
+    greet(sibling)
+    pl.when(has_right)(lambda: greet(ahead))
+    pl.when(has_left)(lambda: greet(behind))
+    pl.when(has_far)(lambda: greet(far))
+    more = [cond.astype(jnp.int32) for cond in (has_right, has_left, has_far)]
+    pl.semaphore_wait(barrier, 4 + more[0] + more[1] + more[2])
+
+    send_own(0)
+
+    def norm_rows(i, carry):
+        rows = pl.ds(pl.multiple_of(i * 32, 32), 32)
+        mod[h, rows, :] = modulate(tokens[rows, :].astype(jnp.float32), shift[...], scale[...])
+        return carry
+
+    def piece(tile, part):
+        return mod.at[tile, pl.ds(part * half, half)]
+
+    def token_copy(peer, tile, part):
+        return remote(
+            piece(tile, part), piece(tile, part), t_send.at[peer, part], t_recv.at[peer, part],
+            (peers[peer], w),
+        )
+
+    def token_forward(peer, part):
+        tile = peers[3 - peer]
+        return remote(
+            piece(tile, part), piece(tile, part), f_send.at[part], t_recv.at[3, part],
+            (peers[peer], w),
+        )
+
+    lax.fori_loop(0, half // 32, norm_rows, 0)
+    send(token_copy(1, h, 0))
+    lax.fori_loop(half // 32, count // 32, norm_rows, 0)
+    send(token_copy(2, h, 1))
+    send(token_copy(1, h, 1))
+    send(token_copy(2, h, 0))
+    send_own(1)
+    forward(0, 1)
+    send_own(2)
+    for d in range(2, deep):
+        forward(0, d)
+    token_copy(1, peers[1], 0).wait_recv()
+    send(token_forward(2, 0))
+    token_copy(2, peers[2], 1).wait_recv()
+    send(token_forward(1, 1))
+    for d in range(1, deep):
+        forward(1, d)
+    send_own(3)
+    whole(0)
+    whole(1)
+
+    def heads_norm(raw, gain):
+        parts = [per_head_norm(raw[:, i * HD : (i + 1) * HD], gain) for i in range(each)]
+        return jnp.concatenate(parts, axis=1)
+
+    def halo(j, side):
+        tile = peers[j]
+        rows = pl.ds(pl.multiple_of(tile * count, 16), count)
+        left = jnp.where(c == 0, side, 1 - side)
+        return remote(
+            kv.at[1, :, rows], kv.at[2 * left, :, rows], kv_send.at[side, j], kv_recv.at[side, j],
+            far if side else sibling,
+        )
+
+    def keys_of(j):
+        tile = peers[j]
+        rows = pl.ds(pl.multiple_of(tile * count, 16), count)
+        left = mod[tile]
+        kv[1, 0, rows, :] = heads_norm(add_rows(left, wbuf[0]), k_gain[...])
+        kv[1, 1, rows, :] = add_rows(left, wbuf[1]).astype(jnp.bfloat16)
+        send(halo(j, 1), has_far)
+        send(halo(j, 0))
+
+    keys_of(0)
+    forward(2, 1)
+    token_copy(1, peers[1], 1).wait_recv()
+    keys_of(1)
+    if deep > 2:
+        forward(2, 2)
+    token_copy(2, peers[2], 0).wait_recv()
+    keys_of(2)
+    for d in range(3, deep):
+        forward(2, d)
+    token_forward(1, 0).wait_recv()
+    token_forward(1, 1).wait_recv()
+    keys_of(3)
+    whole(2)
+    for t in range(len(peers)):
+        rows = pl.ds(t * count, count)
+        query[rows, :] = heads_norm(add_rows(mod[t], wbuf[2]), q_gain[...])
+    tiles = len(peers)
+
+    def attend(place, t, first):
+        low, high = max(t - 1, 0), min(t + 2, tiles)
+        rows = pl.ds(low * count, (high - low) * count)
+
+        def one_head(i, carry):
+            columns = pl.ds(pl.multiple_of(i * HD, HD), HD)
+            state = None
+            if not first:
+                state = (tops[i, t, :, :1], totals[i, t, :, :1], sums[i, t])
+            top, total, summed = softmax_step(
+                state,
+                query[pl.ds(t * count, count), columns],
+                kv[place, 0, rows, columns],
+                kv[place, 1, rows, columns],
+            )
+            tops[i, t] = jnp.broadcast_to(top, (count, HD))
+            totals[i, t] = jnp.broadcast_to(total, (count, HD))
+            sums[i, t] = summed
+            return carry
+
+        lax.fori_loop(0, each, one_head, 0)
+
+    def out_copy(j, tile, part):
+        rows = pl.ds(pl.multiple_of(part * (inner // 2), 16), inner // 2)
+        return obuf.at[tile, rows]
+
+    def out_share(j):
+        block = out_copy(j, h, c)
+        return remote(block, block, o_send.at[j], o_recv.at[j], (peers[j], w))
+
+    def out_sibling(j, part):
+        block = out_copy(j, peers[j], part)
+        return remote(block, block, os_send.at[j], os_recv.at[j], sibling)
+
+    for t in range(tiles):
+        attend(1, t, True)
+        if 1 <= t < deep:
+            forward(3, t)
+    for d in range(tiles, deep):
+        forward(3, d)
+    whole(3)
+    for j in range(1, tiles):
+        send(out_share(j))
+    for j in range(tiles):
+        halo(j, 0).wait_recv()
+    for t in range(tiles):
+        attend(2 - 2 * c, t, False)
+    for j in range(tiles):
+        pl.when(has_far)(halo(j, 1).wait_recv)
+
+    def attended_copy(tile, source, slot):
+        rows = pl.ds(pl.multiple_of(tile * count, 16), count)
+        columns = pl.ds(pl.multiple_of(source * mine, HD), mine)
+        return remote(
+            attended.at[rows], gathered.at[:, columns], a_send.at[slot], a_recv.at[source], (tile, w)
+        )
+
+    for t in range(tiles):
+        pl.when(has_far)(lambda: attend(2 * c, t, False))
+        parts = [(sums[i, t] / totals[i, t]).astype(jnp.bfloat16) for i in range(each)]
+        block = jnp.concatenate(parts, axis=1)
+        attended[pl.ds(t * count, count), :] = block
+        send(attended_copy(t, h, t), h != t)
+
+        def keep():
+            gathered[:, pl.ds(pl.multiple_of(h * mine, HD), mine)] = block
+
+        pl.when(h == t)(keep)
+
+    for j in range(1, tiles):
+        out_copy_in = remote(
+            out_copy(j, peers[j], c), out_copy(j, peers[j], c), o_send.at[j], o_recv.at[j],
+            (peers[j], w),
+        )
+        out_copy_in.wait_recv()
+        send(out_sibling(j, c))
+    for s in range(tiles):
+        pl.when(h != s)(attended_copy(h, s, s).wait_recv)
+    for j in range(1, tiles):
+        out_sibling(j, 1 - c).wait_recv()
+    for q in range(tiles):
+        columns = slice(q * mine, (q + 1) * mine)
+        update[:, columns] = (gate[:, columns] * add_rows(gathered[...], obuf[q])).astype(
+            jnp.bfloat16
+        )
+    for copy, cond in pending:
+        if cond is None:
+            copy.wait_send()
+        else:
+            pl.when(cond)(copy.wait_send)
+
+
+def shards_heads(tokens, shift, scale, gate, qkv_weight, out_weight, q_gain, k_gain):
+    tall, wide = lax.axis_size("ha"), lax.axis_size("wa")
+    each = HEADS // tall
+    inner, mine = HEADS * HD, HEADS // tall * HD
+    width = tokens.shape[-1]
+    flat = tokens.reshape(-1, width)
+    count = flat.shape[0]
+    vmem = pl.BlockSpec(memory_space=pltpu.VMEM)
+    hbm = pl.BlockSpec(memory_space=pl.ANY)
+    dma = pltpu.SemaphoreType.DMA
+    state = pltpu.VMEM((each, tall, count, HD), jnp.float32)
+    update = pl.pallas_call(
+        lambda *refs: block_kernel(wide, *refs),
+        out_shape=jax.ShapeDtypeStruct((count, width), jnp.bfloat16),
+        in_specs=[vmem, vmem, vmem, vmem, hbm, hbm, vmem, vmem],
+        out_specs=vmem,
+        scratch_shapes=[
+            pltpu.VMEM((tall, count, width), jnp.bfloat16),
+            pltpu.VMEM((3, width, mine), jnp.bfloat16),
+            pltpu.VMEM((tall, inner, mine), jnp.bfloat16),
+            pltpu.VMEM((tall * count, mine), jnp.bfloat16),
+            pltpu.VMEM((3, 2, tall * count, mine), jnp.bfloat16),
+            pltpu.VMEM((tall * count, mine), jnp.bfloat16),
+            pltpu.VMEM((count, inner), jnp.bfloat16),
+            state,
+            state,
+            state,
+            dma((4,)),
+            dma((4, wide, 3)),
+            dma((4, wide)),
+            dma((3, 2)),
+            dma((4, 2)),
+            dma((2,)),
+            dma((2, tall)),
+            dma((2, tall)),
+            dma((tall,)),
+            dma((tall,)),
+            dma((tall,)),
+            dma((tall,)),
+            dma((tall,)),
+            dma((tall,)),
+        ],
+        compiler_params=pltpu.CompilerParams(
+            collective_id=0, has_side_effects=True, vmem_limit_bytes=56 * 2**20
+        ),
+        cost_estimate=pl.CostEstimate(
+            flops=9 * 10**9, bytes_accessed=4 * 10**6, transcendentals=6 * 10**6
+        ),
+        name="block",
+    )(flat, shift[None], scale[None], gate[None], qkv_weight, out_weight, q_gain[None], k_gain[None])
+    return update.reshape(tokens.shape)
+
+
+def shards(tokens, *rest):
+    plain = lax.axis_size("ha") != 4 or lax.axis_size("wa") % 2 or tokens.shape[0] != TILE_T
+    return (shards_general if plain else shards_heads)(tokens, *rest)
+
+
 def solution(mesh):
     return jax.shard_map(
         shards,

time: 452 us -> 108 us (0.24)
  the two profiles are of different devices: /device:TPU:12 before, /device:TPU:0 now
where the time goes in v1:
time: 108 us
  Pallas kernels  102 us (94%)
  local copies, waits for them, and re-layouts  5.94 us (6%)
    pallas_call x1, Pallas kernels, shards_heads(): pl.pallas_call(lambda *refs: block_kernel(wide, *refs), out_shape=jax.Sha...  102 us

profile of v1, /device:TPU:0, one launch (start us, length us, event | category | flops | bytes accessed | tf_op | source)
XLA Modules:
  0.0 108.1 jit_solution(8463288768684286063)
XLA Ops:
  0.0 1.3 %broadcast_in_dim.15.refs_1_ = f32[1,1536]{1,0:T(1,128)} reshape(f32[1536]{0:T(1024)} %param.9) | data formatting | bytes 12288 | tf_op jit(solution)/shard_map/broadcast_in_dim | solution.py:447
  1.3 1.3 %broadcast_in_dim.16.refs_2_ = f32[1,1536]{1,0:T(1,128)} reshape(f32[1536]{0:T(1024)} %param.10) | data formatting | bytes 12288 | tf_op jit(solution)/shard_map/broadcast_in_dim | solution.py:447
  2.6 1.3 %broadcast_in_dim.17.refs_3_ = f32[1,1536]{1,0:T(1,128)} reshape(f32[1536]{0:T(1024)} %param.11) | data formatting | bytes 12288 | tf_op jit(solution)/shard_map/broadcast_in_dim | solution.py:447
  3.9 102.1 %block.1 = bf16[256,1536]{1,0:T(8,128)(2,1)} custom-call(bf16[256,1536]{1,0:T(8,128)(2,1)} %bitcast.5, f32[1,1536]{1,0:T(1,128)} %broadcast_in_dim.15.refs_1_, f32[1,1536]{1,0:T(1,128)} %broadcast_in_dim.16.refs_2_, f32[1,1536]{1,0:T(1,128)} %broadcast_in_dim.17.refs_3_, bf16[192,4608]{1,0:T(8,128)(2,1)} %refs_4_.1, bf16[192,1536]{1,0:T(8,128)(2,1)} %refs_5_.1, ...), custom_call_target="tpu_custom_call" | custom-call | flops 8999999488 | bytes 4000000 | tf_op jit(solution)/shard_map/block/pallas_call | solution.py:409
  106.0 2.1 %copy.10 = bf16[4,8,8,1536]{3,2,1,0:T(8,128)(2,1)} copy(bf16[4,8,8,1536]{3,2,1,0:T(8,128)(2,1)} %bitcast.4) | data formatting | bytes 1572864

commit v2 on v1

--- a/solution.py
+++ b/solution.py
@@ -130,7 +130,7 @@
     wide, tokens, shift, scale, gate, qkv_weight, out_weight, q_gain, k_gain, update,
     mod, wbuf, obuf, query, kv, attended, gathered, tops, totals, sums,
     load_sem, w_send, w_recv, t_send, t_recv, f_send, kv_send, kv_recv,
-    o_send, o_recv, os_send, os_recv, a_send, a_recv,
+    o_send, o_recv, of_send, of_recv, os_send, os_recv, a_send, a_recv,
 ):
     h, w = lax.axis_index("ha"), lax.axis_index("wa")
     z, c = lax.div(w, 2), lax.rem(w, 2)
@@ -163,8 +163,9 @@
         pending.append((copy, cond))
 
     def slot(kind, source):
-        rows = pl.ds(pl.multiple_of(source * depth, 16), depth)
-        return obuf.at[h, rows] if kind == 3 else wbuf.at[kind, rows]
+        if kind == 3:
+            return obuf.at[h, lax.div(source, 2), lax.rem(source, 2)]
+        return wbuf.at[kind, pl.ds(pl.multiple_of(source * depth, 16), depth)]
 
     def load(kind):
         if kind == 3:
@@ -185,6 +186,15 @@
         send(pass_on(kind, 0, 0, ahead, w), has_right)
         send(pass_on(kind, 0, 1, behind, w), has_left)
         send(pass_on(kind, 0, 2, sibling, w))
+        if kind == 3:
+            share_out(w, None)
+
+    def share_out(source, cond):
+        block, layer = slot(3, source), lax.div(source, 2)
+        for j in (1, 2):
+            send(
+                remote(block, block, o_send.at[j, layer], o_recv.at[j, layer], (peers[j], w)), cond
+            )
 
     def forward(kind, d):
         from_left, from_right = z >= d, z < deep - d
@@ -192,10 +202,14 @@
         pl.when(from_left)(pass_on(kind, 2 * d - 1, 2, sibling, source).wait_recv)
         send(pass_on(kind, 2 * d - 1, 0, ahead, source), from_left & has_right)
         send(pass_on(kind, 2 * d - 1, 2, sibling, source), from_left)
+        if kind == 3:
+            share_out(source, from_left)
         source = w + 2 * d
         pl.when(from_right)(pass_on(kind, 2 * d, 2, sibling, source).wait_recv)
         send(pass_on(kind, 2 * d, 1, behind, source), from_right & has_left)
         send(pass_on(kind, 2 * d, 2, sibling, source), from_right)
+        if kind == 3:
+            share_out(source, from_right)
 
     def whole(kind):
         for i in range(deep):
@@ -294,9 +308,12 @@
     keys_of(2)
     for d in range(3, deep):
         forward(2, d)
+    forward(3, 1)
     token_forward(1, 0).wait_recv()
     token_forward(1, 1).wait_recv()
     keys_of(3)
+    if deep > 2:
+        forward(3, 2)
     whole(2)
     for t in range(len(peers)):
         rows = pl.ds(t * count, count)
@@ -307,8 +324,8 @@
         low, high = max(t - 1, 0), min(t + 2, tiles)
         rows = pl.ds(low * count, (high - low) * count)
 
-        def one_head(i, carry):
-            columns = pl.ds(pl.multiple_of(i * HD, HD), HD)
+        for i in range(each):
+            columns = pl.ds(i * HD, HD)
             state = None
             if not first:
                 state = (tops[i, t, :, :1], totals[i, t, :, :1], sums[i, t])
@@ -321,35 +338,34 @@
             tops[i, t] = jnp.broadcast_to(top, (count, HD))
             totals[i, t] = jnp.broadcast_to(total, (count, HD))
             sums[i, t] = summed
-            return carry
-
-        lax.fori_loop(0, each, one_head, 0)
-
-    def out_copy(j, tile, part):
-        rows = pl.ds(pl.multiple_of(part * (inner // 2), 16), inner // 2)
-        return obuf.at[tile, rows]
-
-    def out_share(j):
-        block = out_copy(j, h, c)
-        return remote(block, block, o_send.at[j], o_recv.at[j], (peers[j], w))
-
-    def out_sibling(j, part):
-        block = out_copy(j, peers[j], part)
+
+    def out_forward(peer, part):
+        first, size = (0, deep // 2) if part == 0 else (deep // 2, deep - deep // 2)
+        block = obuf.at[peers[3 - peer], pl.ds(first, size), c]
+        return remote(block, block, of_send.at[part], of_recv.at[part], (peers[peer], w))
+
+    def out_sibling(j, core):
+        block = obuf.at[peers[j], :, core]
         return remote(block, block, os_send.at[j], os_recv.at[j], sibling)
 
+    for d in range(3, deep):
+        forward(3, d)
     for t in range(tiles):
         attend(1, t, True)
-        if 1 <= t < deep:
-            forward(3, t)
-    for d in range(tiles, deep):
-        forward(3, d)
-    whole(3)
-    for j in range(1, tiles):
-        send(out_share(j))
     for j in range(tiles):
         halo(j, 0).wait_recv()
     for t in range(tiles):
         attend(2 - 2 * c, t, False)
+        if t == 1:
+            for j in (1, 2):
+                for layer in range(deep):
+                    block = obuf.at[peers[j], layer, c]
+                    remote(
+                        block, block, o_send.at[j, layer], o_recv.at[j, layer], (peers[j], w)
+                    ).wait_recv()
+                send(out_forward(3 - j, j - 1))
+            for j in (1, 2):
+                send(out_sibling(j, c))
     for j in range(tiles):
         pl.when(has_far)(halo(j, 1).wait_recv)
 
@@ -372,22 +388,18 @@
 
         pl.when(h == t)(keep)
 
-    for j in range(1, tiles):
-        out_copy_in = remote(
-            out_copy(j, peers[j], c), out_copy(j, peers[j], c), o_send.at[j], o_recv.at[j],
-            (peers[j], w),
-        )
-        out_copy_in.wait_recv()
-        send(out_sibling(j, c))
+    for part in range(2):
+        out_forward(2 - part, part).wait_recv()
+    send(out_sibling(3, c))
+    whole(3)
     for s in range(tiles):
         pl.when(h != s)(attended_copy(h, s, s).wait_recv)
     for j in range(1, tiles):
         out_sibling(j, 1 - c).wait_recv()
     for q in range(tiles):
         columns = slice(q * mine, (q + 1) * mine)
-        update[:, columns] = (gate[:, columns] * add_rows(gathered[...], obuf[q])).astype(
-            jnp.bfloat16
-        )
+        product = add_rows(gathered[...], obuf[q].reshape(inner, mine))
+        update[:, columns] = (gate[columns] * product).astype(jnp.bfloat16)
     for copy, cond in pending:
         if cond is None:
             copy.wait_send()
@@ -414,7 +426,7 @@
         scratch_shapes=[
             pltpu.VMEM((tall, count, width), jnp.bfloat16),
             pltpu.VMEM((3, width, mine), jnp.bfloat16),
-            pltpu.VMEM((tall, inner, mine), jnp.bfloat16),
+            pltpu.VMEM((tall, wide // 2, 2, inner // wide, mine), jnp.bfloat16),
             pltpu.VMEM((tall * count, mine), jnp.bfloat16),
             pltpu.VMEM((3, 2, tall * count, mine), jnp.bfloat16),
             pltpu.VMEM((tall * count, mine), jnp.bfloat16),
@@ -430,8 +442,10 @@
             dma((2,)),
             dma((2, tall)),
             dma((2, tall)),
-            dma((tall,)),
-            dma((tall,)),
+            dma((3, wide // 2)),
+            dma((3, wide // 2)),
+            dma((2,)),
+            dma((2,)),
             dma((tall,)),
             dma((tall,)),
             dma((tall,)),
@@ -444,7 +458,7 @@
             flops=9 * 10**9, bytes_accessed=4 * 10**6, transcendentals=6 * 10**6
         ),
         name="block",
-    )(flat, shift[None], scale[None], gate[None], qkv_weight, out_weight, q_gain[None], k_gain[None])
+    )(flat, shift, scale, gate, qkv_weight, out_weight, q_gain, k_gain)
     return update.reshape(tokens.shape)
 
 

time: 108 us -> 88.3 us (0.82)
  the two profiles are of different devices: /device:TPU:0 before, /device:TPU:6 now
where the time goes in v2:
time: 88.3 us; the launch traced here: 88.1 us
  Pallas kernels  86.1 us (98%)
  local copies, waits for them, and re-layouts  2.06 us (2%)
    pallas_call x1, Pallas kernels, shards_heads(): pl.pallas_call(lambda *refs: block_kernel(wide, *refs), out_shape=jax.Sha...  86.1 us
    unnamed x1, local copies, waits for them, and re-layouts  2.06 us

profile of v2, /device:TPU:6, one launch (start us, length us, event | category | flops | bytes accessed | tf_op | source)
XLA Modules:
  0.0 88.1 jit_solution(3441121333424856212)
XLA Ops:
  0.0 86.1 %block.1 = bf16[256,1536]{1,0:T(8,128)(2,1)} custom-call(bf16[256,1536]{1,0:T(8,128)(2,1)} %bitcast.3, f32[1536]{0:T(1024)} %refs_1_.1, f32[1536]{0:T(1024)} %refs_2_.1, f32[1536]{0:T(1024)} %refs_3_.1, bf16[192,4608]{1,0:T(8,128)(2,1)} %refs_4_.1, bf16[192,1536]{1,0:T(8,128)(2,1)} %refs_5_.1, f32[128]{0:T(128)} %refs_6_.1, f32[128]{0:T(128)} %refs_7_.1), custom_call_target="tpu_custom_call" | custom-call | flops 8999999488 | bytes 4000000 | tf_op jit(solution)/shard_map/block/pallas_call | solution.py:421
  86.1 2.1 %copy.10 = bf16[4,8,8,1536]{3,2,1,0:T(8,128)(2,1)} copy(bf16[4,8,8,1536]{3,2,1,0:T(8,128)(2,1)} %bitcast.2) | data formatting | bytes 1572864
